TPU v7x, 32 devices: a whole 2x2x4 slice. The times are simulated.
32 devices in a mesh: grp: 4 (over z), dp: 8 (over y, x, core).
Axes of the slice: x: 2, y: 2, z: 4, core: 2. Of those that a mesh axis runs over, the one named last changes fastest.
Arguments:
- grads: bfloat16 [4, 8, 8, 8192], P('grp', 'dp'), may hold values from -12 to 12
- momentum: float32 [4, 8, 8, 8192], P('grp', 'dp'), may hold values from -152 to 152
- worker_error: float32 [4, 8, 8, 8192], P('grp', 'dp'), may hold values from -6 to 6
- server_error: float32 [4, 8, 8192], P('grp', 'dp'), may hold values from -2 to 2
Outputs:
- synced: float32 [8, 8192], replicated
- worker_error_out: float32 [4, 8, 8, 8192], P('grp', 'dp')
- server_error_out: float32 [4, 8, 8192], P('grp', 'dp')
All inputs are finite; a program needn't handle non-finite values.
Results may differ from a plain program's by a relative error of at most 0.012.
Values may be sent and summed in bfloat16 or wider, within the bound.
A program may use at most 64 MiB of HBM per device.

v0:
```python
import jax
import jax.numpy as jnp
from jax import lax
from jax.sharding import PartitionSpec as P


def compress(values):
    row_scale = (jnp.mean(jnp.abs(values), axis=-1) + 1e-06).astype(jnp.bfloat16)
    scale_wide = row_scale.astype(jnp.float32)[..., None]
    coded = jnp.tanh(values / scale_wide).astype(jnp.bfloat16)
    leftover = values - scale_wide * coded.astype(jnp.float32)
    return (row_scale, coded, leftover)


def per_device(grads, momentum, worker_error, server_error):
    blended = 0.9 * momentum + 0.1 * grads.astype(jnp.float32) + worker_error
    row_scale, coded, werr_new = compress(blended)
    got_code, got_scale = (
        lax.all_to_all(coded, "dp", split_axis=2, concat_axis=1, tiled=True),
        lax.all_to_all(row_scale, "dp", split_axis=2, concat_axis=1, tiled=True),
    )
    workers = lax.axis_size("dp")
    groups = lax.axis_size("grp")
    summed = jnp.einsum("gwrd,gwr->grd", got_code, got_scale, preferred_element_type=jnp.float32)
    server_input = summed / workers + server_error
    server_scale, server_code, serr_new = compress(server_input)
    decoded = server_scale.astype(jnp.float32)[..., None] * server_code.astype(jnp.float32)
    averaged = lax.psum(decoded.astype(jnp.bfloat16), "grp").astype(jnp.float32) / groups
    synced = lax.all_gather(averaged.astype(jnp.bfloat16), "dp", axis=1, tiled=True).astype(
        averaged.dtype
    )[0]
    return (synced, werr_new, serr_new)


def solution(mesh):
    placed = (
        P("grp", "dp", None, None),
        P("grp", "dp", None, None),
        P("grp", "dp", None, None),
        P("grp", "dp", None),
    )
    return jax.shard_map(
        per_device,
        mesh=mesh,
        in_specs=placed,
        out_specs=(P(), P("grp", "dp", None, None), P("grp", "dp", None)),
        check_vma=False,
    )
```

profile of v0, /device:TPU:0, one launch (start us, length us, event | category | flops | bytes accessed | tf_op | source)
XLA Modules:
  0.0 53.0 jit_solution(12931912794834328799)
XLA Ops:
  0.6 1.3 %abs_reduce_fusion = (f32[8]{0:T(128)S(1)}, f32[1,1,8,8192]{3,2,1,0:T(8,128)S(1)}) fusion(f32[1,1,8,8192]{3,2,1,0:T(8,128)} %param.6, bf16[1,1,8,8192]{3,2,1,0:T(8,128)(2,1)} %param.4, f32[1,1,8,8192]{3,2,1,0:T(8,128)} %param.5), kind=kLoop, calls=%fused_computation.3 | loop fusion | flops 458744 | bytes 917536 | tf_op jit(solution)/shard_map/reduce_sum | solution.py:8
  1.9 0.7 %copy.24 = bf16[1,1,8]{1,0,2:T(2,128)(2,1)} copy(bf16[1,1,8]{2,1,0:T(2,128)(2,1)S(1)} %get-tuple-element.18) | data formatting | bytes 32 | tf_op jit(solution)/shard_map/convert_element_type | solution.py:8
  2.6 5.2 %all-to-all-start.1 = ((bf16[1,1,8]{1,0,2:T(2,128)(2,1)}), bf16[1,1,8]{1,0,2:T(2,128)(2,1)S(1)}, u32[]{:S(2)}, u32[]{:S(2)}) async-start(bf16[1,1,8]{1,0,2:T(2,128)(2,1)} %copy.24), calls=%async_computation.1 | async-start | bytes 8192 | tf_op jit(solution)/shard_map/all_to_all | solution.py:20
  7.8 0.8 %multiply_subtract_fusion = (f32[1,1,8,8192]{3,2,1,0:T(8,128)}, bf16[1,1,8,8192]{3,2,1,0:T(8,128)(2,1)S(1)}) fusion(f32[1,1,8,8192]{3,2,1,0:T(8,128)S(1)} %get-tuple-element.15, f32[8]{0:T(128)S(1)} %get-tuple-element.19), kind=kLoop, calls=%fused_computation.1 | loop fusion | flops 327680 | bytes 655392 | tf_op jit(solution)/shard_map/sub | solution.py:11
  8.6 0.2 copy.36
  8.8 0.5 broadcast.56
  9.3 1.4 %reduce.3 = bf16[8,8192]{1,0:T(8,128)(2,1)S(1)} reduce(bf16[8,1,1,8192]{3,2,1,0:T(2,128)(2,1)S(1)} %bitcast.28, bf16[]{:T(256)} %broadcast.56), dimensions={1,2}, to_apply=%bitcast.27.reduce_sub_computation | reduce | bytes 262146
  10.7 0.7 %reshape.72 = bf16[8,2,4096]{2,1,0:T(2,128)(2,1)} reshape(bf16[8,8192]{1,0:T(8,128)(2,1)S(1)} %reduce.3) | data formatting | bytes 262144
  11.5 0.9 %all-to-all-done.1 = bf16[1,1,8]{1,0,2:T(2,128)(2,1)S(1)} async-done(((bf16[1,1,8]{1,0,2:T(2,128)(2,1)}), bf16[1,1,8]{1,0,2:T(2,128)(2,1)S(1)}, u32[]{:S(2)}, u32[]{:S(2)}) %all-to-all-start.1) | async-done | bytes 48 | tf_op jit(solution)/shard_map/all_to_all | solution.py:20
  12.4 3.4 %all-to-all-start = ((bf16[8,2,4096]{2,1,0:T(2,128)(2,1)}), bf16[8,2,4096]{2,1,0:T(2,128)(2,1)S(1)}, u32[]{:S(2)}, u32[]{:S(2)}) async-start(bf16[8,2,4096]{2,1,0:T(2,128)(2,1)} %reshape.72), calls=%async_computation | async-start | bytes 262144 | tf_op jit(solution)/shard_map/all_to_all | solution.py:19
  15.8 0.1 reduce.2
  15.9 5.3 %all-to-all-done = bf16[8,2,4096]{2,1,0:T(2,128)(2,1)S(1)} async-done(((bf16[8,2,4096]{2,1,0:T(2,128)(2,1)}), bf16[8,2,4096]{2,1,0:T(2,128)(2,1)S(1)}, u32[]{:S(2)}, u32[]{:S(2)}) %all-to-all-start) | async-done | bytes 131104 | tf_op jit(solution)/shard_map/all_to_all | solution.py:19
  21.2 0.1 reshape.73
  21.3 0.3 fusion
  21.6 0.0 copy-start
  21.6 0.7 %copy-done = f32[1,1,8192]{2,1,0:T(1,128)S(1)} copy-done((f32[1,1,8192]{2,1,0:T(1,128)S(1)}, f32[1,1,8192]{2,1,0:T(1,128)}, u32[]{:S(2)}) %copy-start) | copy-done | bytes 32792
  22.4 0.7 %abs_reduce_fusion.1 = f32[]{:T(128)} fusion(f32[1,1,8192]{2,0,1:T(1,128)S(1)} %bitcast.30, f32[1,1,8192]{2,1,0:T(1,128)S(1)} %copy-done), kind=kLoop, calls=%fused_computation.12 | loop fusion | flops 24575 | bytes 65540 | tf_op jit(solution)/shard_map/reduce_sum | solution.py:8
  23.7 0.7 %subtract_bitcast_fusion = (f32[1,1,8192]{2,1,0:T(1,128)}, bf16[1,1,8192]{2,0,1:T(2,128)(2,1)S(1)}) fusion(f32[1,1,8192]{2,0,1:T(1,128)S(1)} %bitcast.31, f32[1,1,8192]{2,1,0:T(1,128)S(1)} %copy-done, f32[]{:T(128)S(6)} %convert_element_type.69), kind=kLoop, calls=%fused_computation.9 | loop fusion | flops 57344 | bytes 114692
  24.4 19.2 %psum.7 = bf16[1,1,8192]{2,0,1:T(2,128)(2,1)S(1)} all-reduce(bf16[1,1,8192]{2,0,1:T(2,128)(2,1)S(1)} %get-tuple-element.13), channel_id=1, replica_groups=mesh['grp'=4,'dp'=8] {'grp'}, use_global_device_ids=true, to_apply=%region_2.0 | all-reduce | flops 8192 | bytes 32768 | tf_op jit(solution)/shard_map/psum | solution.py:28
  43.7 8.5 %all_gather.3 = bf16[1,8,8192]{2,0,1:T(2,128)(2,1)S(1)} all-gather(bf16[1,1,8192]{2,0,1:T(2,128)(2,1)S(1)} %multiply_convert_fusion), channel_id=1, replica_groups=mesh['grp'=4,'dp'=8] {'dp'}, dimensions={1}, use_global_device_ids=true | all-gather | bytes 147456 | tf_op jit(solution)/shard_map/all_gather | solution.py:29
  52.2 0.9 %copy.35 = f32[1,8,8192]{2,1,0:T(8,128)} copy(bf16[1,8,8192]{2,0,1:T(2,128)(2,1)S(1)} %all_gather.3) | data formatting | bytes 393216
  (3 shorter events, 0.1 us)
Async XLA Ops:
  2.6 9.8 %all-to-all-start.1 = ((bf16[1,1,8]{1,0,2:T(2,128)(2,1)}), bf16[1,1,8]{1,0,2:T(2,128)(2,1)S(1)}, u32[]{:S(2)}, u32[]{:S(2)}) async-start(bf16[1,1,8]{1,0,2:T(2,128)(2,1)} %copy.24), calls=%async_computation.1 | async-start | bytes 8192 | tf_op jit(solution)/shard_map/all_to_all | solution.py:20
  12.4 8.8 %all-to-all-start = ((bf16[8,2,4096]{2,1,0:T(2,128)(2,1)}), bf16[8,2,4096]{2,1,0:T(2,128)(2,1)S(1)}, u32[]{:S(2)}, u32[]{:S(2)}) async-start(bf16[8,2,4096]{2,1,0:T(2,128)(2,1)} %reshape.72), calls=%async_computation | async-start | bytes 262144 | tf_op jit(solution)/shard_map/all_to_all | solution.py:19
  21.6 0.8 %copy-start = (f32[1,1,8192]{2,1,0:T(1,128)S(1)}, f32[1,1,8192]{2,1,0:T(1,128)}, u32[]{:S(2)}) copy-start(f32[1,1,8192]{2,1,0:T(1,128)} %param.7) | copy-start | bytes 98308
where the time goes:
time: 53.4 us; the launch traced here: 53 us
  blocking collectives  27.7 us (52%)
  starting transfers between devices  8.54 us (16%)
  waiting for transfers between devices  6.21 us (12%)
  other arithmetic  5.05 us (9%)
  local copies, waits for them, and re-layouts  3.87 us (7%)
  between operations  1.34 us (3%)
    psum x1, blocking collectives, per_device(): lax.psum(decoded.astype(jnp.bfloat16), 'grp').astype(jnp.float32) / groups  19.2 us
    all_gather x1, blocking collectives, per_device(): lax.all_gather(averaged.astype(jnp.bfloat16), 'dp', axis=1, tiled=True)  8.48 us
    all_to_all x1, waiting for transfers between devices, per_device(): lax.all_to_all(coded, 'dp', split_axis=2, concat_axis=1, tiled=True)  5.31 us
    all_to_all x1, starting transfers between devices, per_device(): lax.all_to_all(row_scale, 'dp', split_axis=2, concat_axis=1, tiled=True)  5.17 us
    all_to_all x1, starting transfers between devices, per_device(): lax.all_to_all(coded, 'dp', split_axis=2, concat_axis=1, tiled=True)  3.37 us
    unnamed x6, local copies, waits for them, and re-layouts  2.97 us
    unnamed x2, other arithmetic  2.09 us
    reduce_sum x2, other arithmetic, compress(): jnp.mean(jnp.abs(values), axis=-1) + 1e-06  1.95 us
  transfers between devices with their start and end apart: 2, of which 2 were waited for; matrix products, arithmetic and copies ran while one was open for 7% of the time, Pallas kernels for 0%

commit v1 on v0

v1 whole, which is shorter than its diff:
```python
import functools

import jax
import jax.numpy as jnp
from jax import lax
from jax.experimental import pallas as pl
from jax.experimental.pallas import tpu as pltpu
from jax.sharding import PartitionSpec as P

MESH = pl.DeviceIdType.MESH
LANES = 128


def each(count, body):
    if count <= 8:
        for k in range(1, count):
            body(k)
    else:
        lax.fori_loop(1, count, lambda k, _: (body(k), None)[1], None)


def wait_bytes(ref, sem):
    pltpu.make_async_copy(ref, ref, sem).wait()


def kernel(
    n, groups, rows, width,
    grads, momentum, worker_error, server_error,
    synced, werr_out, serr_out,
    g_in, m_in, e_in, se_in, blend, code, by_row, werr_st, serr_st, sync_st,
    send, got, scale_send, scale_got, zbuf, gathered,
    in_sem, out_sem, code_sem, scale_sem, z_sem, ag_sem,
):
    me, grp = lax.axis_index("dp"), lax.axis_index("grp")
    tiles = width // LANES

    loads = [
        pltpu.make_async_copy(src, dst, in_sem.at[i])
        for i, (src, dst) in enumerate(
            ((momentum, m_in), (worker_error, e_in), (grads, g_in), (server_error, se_in))
        )
    ]
    for load in loads:
        load.start()

    barrier = pltpu.get_barrier_semaphore()

    def greet_dp(k):
        pl.semaphore_signal(
            barrier, inc=1, device_id=(grp, lax.rem(me + k, n)), device_id_type=MESH
        )

    def greet_grp(k):
        pl.semaphore_signal(
            barrier, inc=1, device_id=(lax.rem(grp + k, groups), me), device_id_type=MESH
        )

    each(n, greet_dp)
    each(groups, greet_grp)

    for load in loads[:3]:
        load.wait()

    total = jnp.zeros((rows, LANES), jnp.float32)
    for t in range(tiles):
        cols = slice(t * LANES, (t + 1) * LANES)
        b = 0.9 * m_in[:, cols] + 0.1 * g_in[:, cols].astype(jnp.float32) + e_in[:, cols]
        blend[:, cols] = b
        total = total + jnp.abs(b)
    mean = jnp.sum(total, axis=1, keepdims=True) / width
    scale = (mean + 1e-6).astype(jnp.bfloat16).astype(jnp.float32)
    inverse = jnp.broadcast_to(1.0 / scale, (rows, LANES))
    scale = jnp.broadcast_to(scale, (rows, LANES))
    for r in range(rows):
        scale_send[r] = scale[r : r + 1]

    pl.semaphore_wait(barrier, n - 1 + groups - 1)

    def send_scale(k):
        to = lax.rem(me + k, n)
        pltpu.make_async_remote_copy(
            src_ref=scale_send.at[to],
            dst_ref=scale_got.at[k - 1],
            send_sem=scale_sem.at[0],
            recv_sem=scale_sem.at[1],
            device_id=(grp, to),
            device_id_type=MESH,
        ).start()

    each(n, send_scale)

    for t in range(tiles):
        cols = slice(t * LANES, (t + 1) * LANES)
        c = jnp.tanh(blend[:, cols] * inverse).astype(jnp.bfloat16).astype(jnp.float32)
        code[:, cols] = c
        by_row[pl.ds(t, rows, stride=tiles), :] = c

    def row_of(r):
        return pl.ds(pl.multiple_of(r * tiles, tiles), tiles)

    def send_code(k):
        to = lax.rem(me + k, n)
        send[k - 1] = by_row[row_of(to), :].astype(jnp.bfloat16)
        pltpu.make_async_remote_copy(
            src_ref=send.at[k - 1],
            dst_ref=got.at[k - 1],
            send_sem=code_sem.at[0],
            recv_sem=code_sem.at[1],
            device_id=(grp, to),
            device_id_type=MESH,
        ).start()

    each(n, send_code)

    for t in range(tiles):
        cols = slice(t * LANES, (t + 1) * LANES)
        werr_st[:, cols] = blend[:, cols] - scale * code[:, cols]
    werr_store = pltpu.make_async_copy(werr_st, werr_out, out_sem.at[0])
    werr_store.start()
    loads[3].wait()

    summed = by_row[row_of(me), :] * scale_send[me]
    wait_bytes(scale_got, scale_sem.at[1])
    wait_bytes(got, code_sem.at[1])
    for k in range(n - 1):
        summed = summed + got[k].astype(jnp.float32) * scale_got[k]
    entry = summed / n + se_in[...]
    mean = jnp.sum(jnp.sum(jnp.abs(entry), axis=0, keepdims=True), axis=1, keepdims=True) / width
    s_scale = (mean + 1e-6).astype(jnp.bfloat16).astype(jnp.float32)
    s_code = jnp.tanh(entry * (1.0 / s_scale)).astype(jnp.bfloat16).astype(jnp.float32)
    decoded = s_scale * s_code
    zbuf[grp] = decoded.astype(jnp.bfloat16)

    def send_z(k):
        pltpu.make_async_remote_copy(
            src_ref=zbuf.at[grp],
            dst_ref=zbuf.at[grp],
            send_sem=z_sem.at[0],
            recv_sem=z_sem.at[1],
            device_id=(lax.rem(grp + k, groups), me),
            device_id_type=MESH,
        ).start()

    each(groups, send_z)
    serr_st[...] = entry - decoded
    serr_store = pltpu.make_async_copy(serr_st, serr_out, out_sem.at[1])
    serr_store.start()

    if groups > 1:
        wait_bytes(zbuf.at[pl.ds(0, groups - 1)], z_sem.at[1])
    mixed = zbuf[0].astype(jnp.float32)
    for g in range(1, groups):
        mixed = mixed + zbuf[g].astype(jnp.float32)
    gathered[me] = (mixed / groups).astype(jnp.bfloat16)

    def send_ag(k):
        pltpu.make_async_remote_copy(
            src_ref=gathered.at[me],
            dst_ref=gathered.at[me],
            send_sem=ag_sem.at[0],
            recv_sem=ag_sem.at[1],
            device_id=(grp, lax.rem(me + k, n)),
            device_id_type=MESH,
        ).start()

    each(n, send_ag)
    wait_bytes(gathered.at[pl.ds(0, n - 1)], ag_sem.at[1])
    for r in range(n):
        by_row[r * tiles : (r + 1) * tiles, :] = gathered[r].astype(jnp.float32)
    for t in range(tiles):
        sync_st[:, t * LANES : (t + 1) * LANES] = by_row[pl.ds(t, rows, stride=tiles), :]
    sync_store = pltpu.make_async_copy(sync_st, synced, out_sem.at[2])
    sync_store.start()

    wait_bytes(scale_got, scale_sem.at[0])
    wait_bytes(got, code_sem.at[0])
    if groups > 1:
        wait_bytes(zbuf.at[pl.ds(0, groups - 1)], z_sem.at[0])
    wait_bytes(gathered.at[pl.ds(0, n - 1)], ag_sem.at[0])
    werr_store.wait()
    serr_store.wait()
    sync_store.wait()


def solution(mesh):
    n, groups = mesh.shape["dp"], mesh.shape["grp"]

    def per_device(grads, momentum, worker_error, server_error):
        rows, width = grads.shape[2:]
        assert rows == n
        tiles = width // LANES
        f32, bf16 = jnp.float32, jnp.bfloat16
        whole = (rows, width)
        block = (tiles, LANES)
        anywhere = pl.BlockSpec(memory_space=pl.ANY)
        synced, werr, serr = pl.pallas_call(
            functools.partial(kernel, n, groups, rows, width),
            out_shape=(
                jax.ShapeDtypeStruct(whole, f32),
                jax.ShapeDtypeStruct(whole, f32),
                jax.ShapeDtypeStruct(block, f32),
            ),
            in_specs=[anywhere] * 4,
            out_specs=(anywhere,) * 3,
            scratch_shapes=[
                pltpu.VMEM(whole, bf16),
                pltpu.VMEM(whole, f32),
                pltpu.VMEM(whole, f32),
                pltpu.VMEM(block, f32),
                pltpu.VMEM(whole, f32),
                pltpu.VMEM(whole, f32),
                pltpu.VMEM((rows * tiles, LANES), f32),
                pltpu.VMEM(whole, f32),
                pltpu.VMEM(block, f32),
                pltpu.VMEM(whole, f32),
                pltpu.VMEM((n - 1,) + block, bf16),
                pltpu.VMEM((n - 1,) + block, bf16),
                pltpu.VMEM((n, 1, LANES), f32),
                pltpu.VMEM((n - 1, 1, LANES), f32),
                pltpu.VMEM((groups,) + block, bf16),
                pltpu.VMEM((n,) + block, bf16),
                pltpu.SemaphoreType.DMA((4,)),
                pltpu.SemaphoreType.DMA((3,)),
                pltpu.SemaphoreType.DMA((2,)),
                pltpu.SemaphoreType.DMA((2,)),
                pltpu.SemaphoreType.DMA((2,)),
                pltpu.SemaphoreType.DMA((2,)),
            ],
            compiler_params=pltpu.CompilerParams(
                collective_id=0, has_side_effects=True, vmem_limit_bytes=48 * 2**20
            ),
            name="sync",
        )(
            grads.reshape(whole),
            momentum.reshape(whole),
            worker_error.reshape(whole),
            server_error.reshape(block),
        )
        return synced, werr.reshape(momentum.shape), serr.reshape(server_error.shape)

    placed = (
        P("grp", "dp", None, None),
        P("grp", "dp", None, None),
        P("grp", "dp", None, None),
        P("grp", "dp", None),
    )
    return jax.shard_map(
        per_device,
        mesh=mesh,
        in_specs=placed,
        out_specs=(P(), P("grp", "dp", None, None), P("grp", "dp", None)),
        check_vma=False,
    )
```

time: 53.4 us -> 23.5 us (0.44)
  blocking collectives: 27.7 us -> 0 us
  Pallas kernels: 0 us -> 17 us
  starting transfers between devices: 8.54 us -> 0 us
  waiting for transfers between devices: 6.21 us -> 0 us
  other arithmetic: 5.05 us -> 0 us
  local copies, waits for them, and re-layouts: 3.87 us -> 5.58 us
  between operations: 1.34 us -> 0.65 us
    psum x1 -> x0, blocking collectives: 19.2 us -> none  [per_device(): lax.psum(decoded.astype(jnp.bfloat16), 'grp').astype(jnp.float32) / groups]
    pallas_call x0 -> x1, Pallas kernels: none -> 17 us  [per_device(): pl.pallas_call(functools.partial(kernel, n, groups, rows, width), out_sha...]
    all_to_all x2 -> x0, starting transfers between devices: 8.54 us -> none  [the longest x1 5.17 us: per_device(): lax.all_to_all(row_scale, 'dp', split_axis=2, concat_axis=1, tiled=True)]
    all_gather x1 -> x0, blocking collectives: 8.48 us -> none  [per_device(): lax.all_gather(averaged.astype(jnp.bfloat16), 'dp', axis=1, tiled=True)]
    all_to_all x2 -> x0, waiting for transfers between devices: 6.21 us -> none  [the longest x1 5.31 us: per_device(): lax.all_to_all(coded, 'dp', split_axis=2, concat_axis=1, tiled=True)]
    unnamed x6 -> x11, local copies, waits for them, and re-layouts: 2.97 us -> 5.58 us
    unnamed x2 -> x0, other arithmetic: 2.09 us -> none
    reduce_sum x2 -> x0, other arithmetic: 1.95 us -> none  [compress(): jnp.mean(jnp.abs(values), axis=-1) + 1e-06]
  transfers between devices with their start and end apart: 2 -> 0, of which waited for: 2 -> 0; matrix products, arithmetic and copies ran while one was open for 7% -> 0% of each run, Pallas kernels for 0% -> 0%
where the time goes in v1:
time: 23.5 us; the launch traced here: 23.2 us
  Pallas kernels  17 us (72%)
  local copies, waits for them, and re-layouts  5.58 us (24%)
  between operations  0.65 us (3%)
    pallas_call x1, Pallas kernels, per_device(): pl.pallas_call(functools.partial(kernel, n, groups, rows, width), out_sha...  17 us
    unnamed x11, local copies, waits for them, and re-layouts  5.58 us

profile of v1, /device:TPU:0, one launch (start us, length us, event | category | flops | bytes accessed | tf_op | source)
XLA Modules:
  0.0 23.2 jit_solution(11210955338698870364)
XLA Ops:
  0.6 0.0 copy-start
  0.6 0.9 %copy-done = f32[1,1,8,8192]{3,2,1,0:T(8,128)S(1)} copy-done((f32[1,1,8,8192]{3,2,1,0:T(8,128)S(1)}, f32[1,1,8,8192]{3,2,1,0:T(8,128)}, u32[]{:S(2)}) %copy-start) | copy-done | bytes 262168
  1.6 0.0 copy-start.1
  1.6 0.9 %copy-done.1 = f32[1,1,8,8192]{3,2,1,0:T(8,128)S(1)} copy-done((f32[1,1,8,8192]{3,2,1,0:T(8,128)S(1)}, f32[1,1,8,8192]{3,2,1,0:T(8,128)}, u32[]{:S(2)}) %copy-start.1) | copy-done | bytes 262168
  2.5 0.0 copy-start.2
  2.5 0.9 %copy-done.2 = bf16[1,1,8,8192]{3,2,1,0:T(8,128)(2,1)S(1)} copy-done((bf16[1,1,8,8192]{3,2,1,0:T(8,128)(2,1)S(1)}, bf16[1,1,8,8192]{3,2,1,0:T(8,128)(2,1)}, u32[]{:S(2)}) %copy-start.2) | copy-done | bytes 131096
  3.4 0.0 copy-start.3
  3.4 0.8 %copy-done.3 = f32[1,1,8192]{2,1,0:T(1,128)S(1)} copy-done((f32[1,1,8192]{2,1,0:T(1,128)S(1)}, f32[1,1,8192]{2,1,0:T(1,128)}, u32[]{:S(2)}) %copy-start.3) | copy-done | bytes 32792
  4.2 17.0 %sync.1 = (f32[8,8192]{1,0:T(8,128)S(1)}, f32[8,8192]{1,0:T(8,128)S(1)}, f32[64,128]{1,0:T(8,128)S(1)}) custom-call(bf16[8,8192]{1,0:T(8,128)(2,1)S(1)} %bitcast.9, f32[8,8192]{1,0:T(8,128)S(1)} %bitcast.6, f32[8,8192]{1,0:T(8,128)S(1)} %bitcast.7, f32[64,128]{1,0:T(8,128)S(1)} %bitcast.11), custom_call_target="tpu_custom_call" | custom-call | tf_op jit(solution)/shard_map/sync/pallas_call | solution.py:196
  21.2 0.7 %copy.10 = f32[8,8192]{1,0:T(8,128)} copy(f32[8,8192]{1,0:T(8,128)S(1)} %get-tuple-element.12) | data formatting | bytes 524288
  21.9 0.7 %copy.11 = f32[1,1,8,8192]{3,2,1,0:T(8,128)} copy(f32[1,1,8,8192]{3,2,1,0:T(8,128)S(1)} %bitcast.8) | data formatting | bytes 524288
  22.6 0.6 %copy.12 = f32[1,1,8192]{2,1,0:T(1,128)} copy(f32[1,1,8192]{2,1,0:T(1,128)S(1)} %bitcast.10) | data formatting | bytes 65536
Async XLA Ops:
  0.6 1.0 %copy-start = (f32[1,1,8,8192]{3,2,1,0:T(8,128)S(1)}, f32[1,1,8,8192]{3,2,1,0:T(8,128)}, u32[]{:S(2)}) copy-start(f32[1,1,8,8192]{3,2,1,0:T(8,128)} %param.5) | copy-start | bytes 786436
  1.6 0.9 %copy-start.1 = (f32[1,1,8,8192]{3,2,1,0:T(8,128)S(1)}, f32[1,1,8,8192]{3,2,1,0:T(8,128)}, u32[]{:S(2)}) copy-start(f32[1,1,8,8192]{3,2,1,0:T(8,128)} %param.6) | copy-start | bytes 786436
  2.5 0.9 %copy-start.2 = (bf16[1,1,8,8192]{3,2,1,0:T(8,128)(2,1)S(1)}, bf16[1,1,8,8192]{3,2,1,0:T(8,128)(2,1)}, u32[]{:S(2)}) copy-start(bf16[1,1,8,8192]{3,2,1,0:T(8,128)(2,1)} %param.4) | copy-start | bytes 393220
  3.4 0.8 %copy-start.3 = (f32[1,1,8192]{2,1,0:T(1,128)S(1)}, f32[1,1,8192]{2,1,0:T(1,128)}, u32[]{:S(2)}) copy-start(f32[1,1,8192]{2,1,0:T(1,128)} %param.7) | copy-start | bytes 98308

commit v2 on v1

--- a/solution.py
+++ b/solution.py
@@ -27,9 +27,9 @@
     n, groups, rows, width,
     grads, momentum, worker_error, server_error,
     synced, werr_out, serr_out,
-    g_in, m_in, e_in, se_in, blend, code, by_row, werr_st, serr_st, sync_st,
+    g_in, m_in, e_in, se_in, blend, code, by_row,
     send, got, scale_send, scale_got, zbuf, gathered,
-    in_sem, out_sem, code_sem, scale_sem, z_sem, ag_sem,
+    in_sem, code_sem, scale_sem, z_sem, ag_sem,
 ):
     me, grp = lax.axis_index("dp"), lax.axis_index("grp")
     tiles = width // LANES
@@ -114,9 +114,7 @@
 
     for t in range(tiles):
         cols = slice(t * LANES, (t + 1) * LANES)
-        werr_st[:, cols] = blend[:, cols] - scale * code[:, cols]
-    werr_store = pltpu.make_async_copy(werr_st, werr_out, out_sem.at[0])
-    werr_store.start()
+        werr_out[:, cols] = blend[:, cols] - scale * code[:, cols]
     loads[3].wait()
 
     summed = by_row[row_of(me), :] * scale_send[me]
@@ -142,9 +140,7 @@
         ).start()
 
     each(groups, send_z)
-    serr_st[...] = entry - decoded
-    serr_store = pltpu.make_async_copy(serr_st, serr_out, out_sem.at[1])
-    serr_store.start()
+    serr_out[...] = entry - decoded
 
     if groups > 1:
         wait_bytes(zbuf.at[pl.ds(0, groups - 1)], z_sem.at[1])
@@ -168,18 +164,24 @@
     for r in range(n):
         by_row[r * tiles : (r + 1) * tiles, :] = gathered[r].astype(jnp.float32)
     for t in range(tiles):
-        sync_st[:, t * LANES : (t + 1) * LANES] = by_row[pl.ds(t, rows, stride=tiles), :]
-    sync_store = pltpu.make_async_copy(sync_st, synced, out_sem.at[2])
-    sync_store.start()
+        synced[:, t * LANES : (t + 1) * LANES] = by_row[pl.ds(t, rows, stride=tiles), :]
 
     wait_bytes(scale_got, scale_sem.at[0])
     wait_bytes(got, code_sem.at[0])
     if groups > 1:
         wait_bytes(zbuf.at[pl.ds(0, groups - 1)], z_sem.at[0])
     wait_bytes(gathered.at[pl.ds(0, n - 1)], ag_sem.at[0])
-    werr_store.wait()
-    serr_store.wait()
-    sync_store.wait()
+
+
+def store(synced, werr, serr, synced_out, werr_out, serr_out, sem):
+    copies = [
+        pltpu.make_async_copy(src, dst, sem.at[i])
+        for i, (src, dst) in enumerate(((synced, synced_out), (werr, werr_out), (serr, serr_out)))
+    ]
+    for copy in copies:
+        copy.start()
+    for copy in copies:
+        copy.wait()
 
 
 def solution(mesh):
@@ -192,7 +194,10 @@
         f32, bf16 = jnp.float32, jnp.bfloat16
         whole = (rows, width)
         block = (tiles, LANES)
+        in_hbm = pl.BlockSpec(memory_space=pltpu.HBM)
+        in_vmem = pl.BlockSpec(memory_space=pltpu.VMEM)
         anywhere = pl.BlockSpec(memory_space=pl.ANY)
+        pinned = functools.partial(pltpu.with_memory_space_constraint, memory_space=pltpu.HBM)
         synced, werr, serr = pl.pallas_call(
             functools.partial(kernel, n, groups, rows, width),
             out_shape=(
@@ -201,7 +206,7 @@
                 jax.ShapeDtypeStruct(block, f32),
             ),
             in_specs=[anywhere] * 4,
-            out_specs=(anywhere,) * 3,
+            out_specs=(in_vmem,) * 3,
             scratch_shapes=[
                 pltpu.VMEM(whole, bf16),
                 pltpu.VMEM(whole, f32),
@@ -210,9 +215,6 @@
                 pltpu.VMEM(whole, f32),
                 pltpu.VMEM(whole, f32),
                 pltpu.VMEM((rows * tiles, LANES), f32),
-                pltpu.VMEM(whole, f32),
-                pltpu.VMEM(block, f32),
-                pltpu.VMEM(whole, f32),
                 pltpu.VMEM((n - 1,) + block, bf16),
                 pltpu.VMEM((n - 1,) + block, bf16),
                 pltpu.VMEM((n, 1, LANES), f32),
@@ -220,7 +222,6 @@
                 pltpu.VMEM((groups,) + block, bf16),
                 pltpu.VMEM((n,) + block, bf16),
                 pltpu.SemaphoreType.DMA((4,)),
-                pltpu.SemaphoreType.DMA((3,)),
                 pltpu.SemaphoreType.DMA((2,)),
                 pltpu.SemaphoreType.DMA((2,)),
                 pltpu.SemaphoreType.DMA((2,)),
@@ -231,11 +232,19 @@
             ),
             name="sync",
         )(
-            grads.reshape(whole),
-            momentum.reshape(whole),
-            worker_error.reshape(whole),
-            server_error.reshape(block),
-        )
+            pinned(grads.reshape(whole)),
+            pinned(momentum.reshape(whole)),
+            pinned(worker_error.reshape(whole)),
+            pinned(server_error.reshape(block)),
+        )
+        synced, werr, serr = pl.pallas_call(
+            store,
+            out_shape=tuple(jax.ShapeDtypeStruct(x.shape, f32) for x in (synced, werr, serr)),
+            in_specs=[anywhere] * 3,
+            out_specs=(in_hbm,) * 3,
+            scratch_shapes=[pltpu.SemaphoreType.DMA((3,))],
+            name="store",
+        )(synced, werr, serr)
         return synced, werr.reshape(momentum.shape), serr.reshape(server_error.shape)
 
     placed = (

time: 23.5 us -> 37.5 us (1.60)
  Pallas kernels: 17 us -> 34.7 us
  local copies, waits for them, and re-layouts: 5.58 us -> 2 us
    pallas_call x0 -> x1, Pallas kernels: none -> 18 us  [per_device(): pl.pallas_call(store, out_shape=tuple((jax.ShapeDtypeStruct(x.shape, f32)...]
    unnamed x11 -> x6, local copies, waits for them, and re-layouts: 5.58 us -> 2 us
where the time goes in v2:
time: 37.5 us; the launch traced here: 37.4 us
  Pallas kernels  34.7 us (93%)
  local copies, waits for them, and re-layouts  2 us (5%)
  between operations  0.65 us (2%)
    pallas_call x1, Pallas kernels, per_device(): pl.pallas_call(store, out_shape=tuple((jax.ShapeDtypeStruct(x.shape, f32)...  18 us
    pallas_call x1, Pallas kernels, per_device(): pl.pallas_call(functools.partial(kernel, n, groups, rows, width), out_sha...  16.7 us
    unnamed x6, local copies, waits for them, and re-layouts  2 us

profile of v2, /device:TPU:0, one launch (start us, length us, event | category | flops | bytes accessed | tf_op | source)
XLA Modules:
  0.0 37.4 jit_solution(11504545149361678634)
XLA Ops:
  0.6 16.7 %sync.1 = (f32[8,8192]{1,0:T(8,128)S(1)}, f32[8,8192]{1,0:T(8,128)S(1)}, f32[64,128]{1,0:T(8,128)S(1)}) custom-call(bf16[8,8192]{1,0:T(8,128)(2,1)} %bitcast.8, f32[8,8192]{1,0:T(8,128)} %bitcast.6, f32[8,8192]{1,0:T(8,128)} %bitcast.7, f32[64,128]{1,0:T(8,128)} %bitcast.9), custom_call_target="tpu_custom_call" | custom-call | tf_op jit(solution)/shard_map/sync/pallas_call | solution.py:201
  17.4 0.0 copy-start
  17.4 0.7 %copy-done = f32[8,8192]{1,0:T(8,128)} copy-done((f32[8,8192]{1,0:T(8,128)}, f32[8,8192]{1,0:T(8,128)S(1)}, u32[]{:S(2)}) %copy-start) | copy-done | bytes 262168
  18.1 0.0 copy-start.1
  18.1 0.7 %copy-done.1 = f32[8,8192]{1,0:T(8,128)} copy-done((f32[8,8192]{1,0:T(8,128)}, f32[8,8192]{1,0:T(8,128)S(1)}, u32[]{:S(2)}) %copy-start.1) | copy-done | bytes 262168
  18.8 0.0 copy-start.2
  18.8 0.6 %copy-done.2 = f32[64,128]{1,0:T(8,128)} copy-done((f32[64,128]{1,0:T(8,128)}, f32[64,128]{1,0:T(8,128)S(1)}, u32[]{:S(2)}) %copy-start.2) | copy-done | bytes 32792
  19.4 18.0 %store.1 = (f32[8,8192]{1,0:T(8,128)}, f32[8,8192]{1,0:T(8,128)}, f32[64,128]{1,0:T(8,128)}) custom-call(f32[8,8192]{1,0:T(8,128)} %copy-done, f32[8,8192]{1,0:T(8,128)} %copy-done.1, f32[64,128]{1,0:T(8,128)} %copy-done.2), custom_call_target="tpu_custom_call" | custom-call | tf_op jit(solution)/shard_map/store/pallas_call | solution.py:240
Async XLA Ops:
  17.4 0.7 %copy-start = (f32[8,8192]{1,0:T(8,128)}, f32[8,8192]{1,0:T(8,128)S(1)}, u32[]{:S(2)}) copy-start(f32[8,8192]{1,0:T(8,128)S(1)} %get-tuple-element.9.synced) | copy-start | bytes 786436
  18.1 0.7 %copy-start.1 = (f32[8,8192]{1,0:T(8,128)}, f32[8,8192]{1,0:T(8,128)S(1)}, u32[]{:S(2)}) copy-start(f32[8,8192]{1,0:T(8,128)S(1)} %get-tuple-element.10.werr) | copy-start | bytes 786436
  18.8 0.6 %copy-start.2 = (f32[64,128]{1,0:T(8,128)}, f32[64,128]{1,0:T(8,128)S(1)}, u32[]{:S(2)}) copy-start(f32[64,128]{1,0:T(8,128)S(1)} %get-tuple-element.11.serr) | copy-start | bytes 98308

commit v3 on v2

--- a/solution.py
+++ b/solution.py
@@ -243,6 +243,7 @@
             in_specs=[anywhere] * 3,
             out_specs=(in_hbm,) * 3,
             scratch_shapes=[pltpu.SemaphoreType.DMA((3,))],
+            compiler_params=pltpu.CompilerParams(vmem_limit_bytes=2**20),
             name="store",
         )(synced, werr, serr)
         return synced, werr.reshape(momentum.shape), serr.reshape(server_error.shape)

time: 37.5 us -> 18.3 us (0.49)
  Pallas kernels: 34.7 us -> 17.6 us
  local copies, waits for them, and re-layouts: 2 us -> 0 us
    pallas_call x1, Pallas kernels: 18 us -> 0.82 us  [per_device(): pl.pallas_call(store, out_shape=tuple((jax.ShapeDtypeStruct(x.shape, f32)...]
    unnamed x6 -> x0, local copies, waits for them, and re-layouts: 2 us -> none
where the time goes in v3:
time: 18.3 us; the launch traced here: 18.2 us
  Pallas kernels  17.6 us (96%)
  between operations  0.64 us (3%)
    pallas_call x1, Pallas kernels, per_device(): pl.pallas_call(functools.partial(kernel, n, groups, rows, width), out_sha...  16.7 us
    pallas_call x1, Pallas kernels, per_device(): pl.pallas_call(store, out_shape=tuple((jax.ShapeDtypeStruct(x.shape, f32)...  0.82 us

profile of v3, /device:TPU:0, one launch (start us, length us, event | category | flops | bytes accessed | tf_op | source)
XLA Modules:
  0.0 18.2 jit_solution(3283633696126113223)
XLA Ops:
  0.6 16.7 %sync.1 = (f32[8,8192]{1,0:T(8,128)S(1)}, f32[8,8192]{1,0:T(8,128)S(1)}, f32[64,128]{1,0:T(8,128)S(1)}) custom-call(bf16[8,8192]{1,0:T(8,128)(2,1)} %bitcast.8, f32[8,8192]{1,0:T(8,128)} %bitcast.6, f32[8,8192]{1,0:T(8,128)} %bitcast.7, f32[64,128]{1,0:T(8,128)} %bitcast.9), custom_call_target="tpu_custom_call" | custom-call | tf_op jit(solution)/shard_map/sync/pallas_call | solution.py:201
  17.4 0.8 %store.1 = (f32[8,8192]{1,0:T(8,128)}, f32[8,8192]{1,0:T(8,128)}, f32[64,128]{1,0:T(8,128)}) custom-call(f32[8,8192]{1,0:T(8,128)S(1)} %get-tuple-element.9.synced, f32[8,8192]{1,0:T(8,128)S(1)} %get-tuple-element.10.werr, f32[64,128]{1,0:T(8,128)S(1)} %get-tuple-element.11.serr), custom_call_target="tpu_custom_call" | custom-call | tf_op jit(solution)/shard_map/store/pallas_call | solution.py:240

commit v4 on v3

v4 whole, which is shorter than its diff:
```python
import functools

import jax
import jax.numpy as jnp
from jax import lax
from jax.experimental import pallas as pl
from jax.experimental.pallas import tpu as pltpu
from jax.sharding import PartitionSpec as P

MESH = pl.DeviceIdType.MESH
LANES = 128


def partners(me, n):
    if n & (n - 1):
        return {k: lax.rem(me + k, n) for k in range(n - 1, 0, -1)}
    flips = [(1 << i, (1 << i) * (1 - 2 * lax.rem(lax.div(me, 1 << i), 2))) for i in range(n.bit_length() - 1)]
    return {k: me + sum(step for bit, step in flips if k & bit) for k in range(n - 1, 0, -1)}


def wait_bytes(ref, sem):
    pltpu.make_async_copy(ref, ref, sem).wait()


def kernel(
    n, groups, rows, width, parts,
    grads, momentum, worker_error, server_error,
    synced, werr_out, serr_out,
    g_in, m_in, e_in, se_in, blend, code, by_row, entry,
    send, got, scale_send, scale_got, zbuf, gathered,
    in_sem, code_sem, scale_sem, z_sem, ag_sem,
):
    me, grp = lax.axis_index("dp"), lax.axis_index("grp")
    tiles = width // LANES
    part = tiles // parts

    loads = [
        pltpu.make_async_copy(src, dst, in_sem.at[i])
        for i, (src, dst) in enumerate(
            ((momentum, m_in), (worker_error, e_in), (grads, g_in), (server_error, se_in))
        )
    ]
    for load in loads:
        load.start()

    mates = partners(me, n)
    others = partners(grp, groups)
    barrier = pltpu.get_barrier_semaphore()
    for to in mates.values():
        pl.semaphore_signal(barrier, inc=1, device_id=(grp, to), device_id_type=MESH)
    for to in others.values():
        pl.semaphore_signal(barrier, inc=1, device_id=(to, me), device_id_type=MESH)

    def push(src, dst, sems, device):
        pltpu.make_async_remote_copy(
            src_ref=src,
            dst_ref=dst,
            send_sem=sems.at[0],
            recv_sem=sems.at[1],
            device_id=device,
            device_id_type=MESH,
        ).start()

    for load in loads[:3]:
        load.wait()

    total = jnp.zeros((rows, LANES), jnp.float32)
    for t in range(tiles):
        cols = slice(t * LANES, (t + 1) * LANES)
        b = 0.9 * m_in[:, cols] + 0.1 * g_in[:, cols].astype(jnp.float32) + e_in[:, cols]
        blend[:, cols] = b
        total = total + jnp.abs(b)
    mean = jnp.sum(total, axis=1, keepdims=True) / width
    scale = (mean + 1e-6).astype(jnp.bfloat16).astype(jnp.float32)
    inverse = jnp.broadcast_to(1.0 / scale, (rows, LANES))
    scale = jnp.broadcast_to(scale, (rows, LANES))
    for r in range(rows):
        scale_send[r] = scale[r : r + 1]

    def block_of(p, r):
        return pl.ds(pl.multiple_of((p * rows + r) * part, part), part)

    for p in range(parts):
        for t in range(part):
            cols = slice((p * part + t) * LANES, (p * part + t + 1) * LANES)
            c = jnp.tanh(blend[:, cols] * inverse).astype(jnp.bfloat16).astype(jnp.float32)
            code[:, cols] = c
            by_row[pl.ds(p * rows * part + t, rows, stride=part), :] = c
        if p == 0:
            pl.semaphore_wait(barrier, n - 1 + groups - 1)
        for k, to in mates.items():
            send[p, k - 1] = by_row[block_of(p, to), :].astype(jnp.bfloat16)
            push(send.at[p, k - 1], got.at[p, k - 1], code_sem.at[p], (grp, to))
        if p == 0:
            for k, to in mates.items():
                push(scale_send.at[to], scale_got.at[k - 1], scale_sem, (grp, to))

    for t in range(tiles):
        cols = slice(t * LANES, (t + 1) * LANES)
        werr_out[:, cols] = blend[:, cols] - scale * code[:, cols]
    loads[3].wait()

    wait_bytes(scale_got, scale_sem.at[1])
    heights = [scale_got[k] for k in range(n - 1)]
    size = jnp.zeros((part, LANES), jnp.float32)
    for p in range(parts):
        here = slice(p * part, (p + 1) * part)
        summed = by_row[block_of(p, me), :] * scale_send[me]
        wait_bytes(got.at[p], code_sem.at[p, 1])
        for k in range(n - 1):
            summed = summed + got[p, k].astype(jnp.float32) * heights[k]
        summed = summed / n + se_in[here, :]
        entry[here, :] = summed
        size = size + jnp.abs(summed)
    mean = jnp.sum(jnp.sum(size, axis=0, keepdims=True), axis=1, keepdims=True) / width
    s_scale = (mean + 1e-6).astype(jnp.bfloat16).astype(jnp.float32)
    s_inverse = 1.0 / s_scale
    for p in range(parts):
        here = slice(p * part, (p + 1) * part)
        s_code = jnp.tanh(entry[here, :] * s_inverse).astype(jnp.bfloat16).astype(jnp.float32)
        decoded = s_scale * s_code
        zbuf[p, grp] = decoded.astype(jnp.bfloat16)
        for to in others.values():
            push(zbuf.at[p, grp], zbuf.at[p, grp], z_sem.at[p], (to, me))
        serr_out[here, :] = entry[here, :] - decoded

    for p in range(parts):
        if groups > 1:
            wait_bytes(zbuf.at[p, pl.ds(0, groups - 1)], z_sem.at[p, 1])
        mixed = zbuf[p, 0].astype(jnp.float32)
        for g in range(1, groups):
            mixed = mixed + zbuf[p, g].astype(jnp.float32)
        gathered[p, me] = (mixed / groups).astype(jnp.bfloat16)
        for to in mates.values():
            push(gathered.at[p, me], gathered.at[p, me], ag_sem.at[p], (grp, to))

    for p in range(parts):
        wait_bytes(gathered.at[p, pl.ds(0, n - 1)], ag_sem.at[p, 1])
        base = p * rows * part
        for r in range(n):
            by_row[base + r * part : base + (r + 1) * part, :] = gathered[p, r].astype(jnp.float32)
        for t in range(part):
            cols = slice((p * part + t) * LANES, (p * part + t + 1) * LANES)
            synced[:, cols] = by_row[pl.ds(base + t, rows, stride=part), :]

    wait_bytes(scale_got, scale_sem.at[0])
    for p in range(parts):
        wait_bytes(got.at[p], code_sem.at[p, 0])
        if groups > 1:
            wait_bytes(zbuf.at[p, pl.ds(0, groups - 1)], z_sem.at[p, 0])
        wait_bytes(gathered.at[p, pl.ds(0, n - 1)], ag_sem.at[p, 0])


def store(synced, werr, serr, synced_out, werr_out, serr_out, sem):
    copies = [
        pltpu.make_async_copy(src, dst, sem.at[i])
        for i, (src, dst) in enumerate(((synced, synced_out), (werr, werr_out), (serr, serr_out)))
    ]
    for copy in copies:
        copy.start()
    for copy in copies:
        copy.wait()


def solution(mesh):
    n, groups = mesh.shape["dp"], mesh.shape["grp"]

    def per_device(grads, momentum, worker_error, server_error):
        rows, width = grads.shape[2:]
        assert rows == n
        tiles = width // LANES
        parts = 2
        part_block = (tiles // parts, LANES)
        f32, bf16 = jnp.float32, jnp.bfloat16
        whole = (rows, width)
        block = (tiles, LANES)
        in_hbm = pl.BlockSpec(memory_space=pltpu.HBM)
        in_vmem = pl.BlockSpec(memory_space=pltpu.VMEM)
        anywhere = pl.BlockSpec(memory_space=pl.ANY)
        pinned = functools.partial(pltpu.with_memory_space_constraint, memory_space=pltpu.HBM)
        synced, werr, serr = pl.pallas_call(
            functools.partial(kernel, n, groups, rows, width, parts),
            out_shape=(
                jax.ShapeDtypeStruct(whole, f32),
                jax.ShapeDtypeStruct(whole, f32),
                jax.ShapeDtypeStruct(block, f32),
            ),
            in_specs=[anywhere] * 4,
            out_specs=(in_vmem,) * 3,
            scratch_shapes=[
                pltpu.VMEM(whole, bf16),
                pltpu.VMEM(whole, f32),
                pltpu.VMEM(whole, f32),
                pltpu.VMEM(block, f32),
                pltpu.VMEM(whole, f32),
                pltpu.VMEM(whole, f32),
                pltpu.VMEM((rows * tiles, LANES), f32),
                pltpu.VMEM(block, f32),
                pltpu.VMEM((parts, n - 1) + part_block, bf16),
                pltpu.VMEM((parts, n - 1) + part_block, bf16),
                pltpu.VMEM((n, 1, LANES), f32),
                pltpu.VMEM((n - 1, 1, LANES), f32),
                pltpu.VMEM((parts, groups) + part_block, bf16),
                pltpu.VMEM((parts, n) + part_block, bf16),
                pltpu.SemaphoreType.DMA((4,)),
                pltpu.SemaphoreType.DMA((parts, 2)),
                pltpu.SemaphoreType.DMA((2,)),
                pltpu.SemaphoreType.DMA((parts, 2)),
                pltpu.SemaphoreType.DMA((parts, 2)),
            ],
            compiler_params=pltpu.CompilerParams(
                collective_id=0, has_side_effects=True, vmem_limit_bytes=48 * 2**20
            ),
            name="sync",
        )(
            pinned(grads.reshape(whole)),
            pinned(momentum.reshape(whole)),
            pinned(worker_error.reshape(whole)),
            pinned(server_error.reshape(block)),
        )
        synced, werr, serr = pl.pallas_call(
            store,
            out_shape=tuple(jax.ShapeDtypeStruct(x.shape, f32) for x in (synced, werr, serr)),
            in_specs=[anywhere] * 3,
            out_specs=(in_hbm,) * 3,
            scratch_shapes=[pltpu.SemaphoreType.DMA((3,))],
            compiler_params=pltpu.CompilerParams(vmem_limit_bytes=2**20),
            name="store",
        )(synced, werr, serr)
        return synced, werr.reshape(momentum.shape), serr.reshape(server_error.shape)

    placed = (
        P("grp", "dp", None, None),
        P("grp", "dp", None, None),
        P("grp", "dp", None, None),
        P("grp", "dp", None),
    )
    return jax.shard_map(
        per_device,
        mesh=mesh,
        in_specs=placed,
        out_specs=(P(), P("grp", "dp", None, None), P("grp", "dp", None)),
        check_vma=False,
    )
```

time: 18.3 us -> 18.4 us (level)
  no operation moved by 1% of the time
where the time goes in v4:
time: 18.4 us; the launch traced here: 18.2 us
  Pallas kernels  17.6 us (96%)
  between operations  0.64 us (3%)
    pallas_call x1, Pallas kernels, per_device(): pl.pallas_call(functools.partial(kernel, n, groups, rows, width, parts),...  16.8 us
    pallas_call x1, Pallas kernels, per_device(): pl.pallas_call(store, out_shape=tuple((jax.ShapeDtypeStruct(x.shape, f32)...  0.82 us

profile of v4, /device:TPU:0, one launch (start us, length us, event | category | flops | bytes accessed | tf_op | source)
XLA Modules:
  0.0 18.2 jit_solution(1000100962807333179)
XLA Ops:
  0.6 16.8 %sync.1 = (f32[8,8192]{1,0:T(8,128)S(1)}, f32[8,8192]{1,0:T(8,128)S(1)}, f32[64,128]{1,0:T(8,128)S(1)}) custom-call(bf16[8,8192]{1,0:T(8,128)(2,1)} %bitcast.8, f32[8,8192]{1,0:T(8,128)} %bitcast.6, f32[8,8192]{1,0:T(8,128)} %bitcast.7, f32[64,128]{1,0:T(8,128)} %bitcast.9), custom_call_target="tpu_custom_call" | custom-call | tf_op jit(solution)/shard_map/sync/pallas_call | solution.py:181
  17.4 0.8 %store.1 = (f32[8,8192]{1,0:T(8,128)}, f32[8,8192]{1,0:T(8,128)}, f32[64,128]{1,0:T(8,128)}) custom-call(f32[8,8192]{1,0:T(8,128)S(1)} %get-tuple-element.9.synced, f32[8,8192]{1,0:T(8,128)S(1)} %get-tuple-element.10.werr, f32[64,128]{1,0:T(8,128)S(1)} %get-tuple-element.11.serr), custom_call_target="tpu_custom_call" | custom-call | tf_op jit(solution)/shard_map/store/pallas_call | solution.py:221

commit v5 on v4

--- a/solution.py
+++ b/solution.py
@@ -1,4 +1,5 @@
 import functools
+import math
 
 import jax
 import jax.numpy as jnp
@@ -16,6 +17,18 @@
         return {k: lax.rem(me + k, n) for k in range(n - 1, 0, -1)}
     flips = [(1 << i, (1 << i) * (1 - 2 * lax.rem(lax.div(me, 1 << i), 2))) for i in range(n.bit_length() - 1)]
     return {k: me + sum(step for bit, step in flips if k & bit) for k in range(n - 1, 0, -1)}
+
+
+def over_tiles(start, count, body, carry=0):
+    batch = math.gcd(count, 8)
+
+    def step(i, held):
+        for j in range(batch):
+            t = start + i * batch + j
+            held = body(t, pl.ds(pl.multiple_of(t * LANES, LANES), LANES), held)
+        return held
+
+    return lax.fori_loop(0, count // batch, step, carry)
 
 
 def wait_bytes(ref, sem):
@@ -64,12 +77,12 @@
     for load in loads[:3]:
         load.wait()
 
-    total = jnp.zeros((rows, LANES), jnp.float32)
-    for t in range(tiles):
-        cols = slice(t * LANES, (t + 1) * LANES)
+    def blend_tile(t, cols, total):
         b = 0.9 * m_in[:, cols] + 0.1 * g_in[:, cols].astype(jnp.float32) + e_in[:, cols]
         blend[:, cols] = b
-        total = total + jnp.abs(b)
+        return total + jnp.abs(b)
+
+    total = over_tiles(0, tiles, blend_tile, jnp.zeros((rows, LANES), jnp.float32))
     mean = jnp.sum(total, axis=1, keepdims=True) / width
     scale = (mean + 1e-6).astype(jnp.bfloat16).astype(jnp.float32)
     inverse = jnp.broadcast_to(1.0 / scale, (rows, LANES))
@@ -81,11 +94,14 @@
         return pl.ds(pl.multiple_of((p * rows + r) * part, part), part)
 
     for p in range(parts):
-        for t in range(part):
-            cols = slice((p * part + t) * LANES, (p * part + t + 1) * LANES)
+
+        def code_tile(t, cols, held):
             c = jnp.tanh(blend[:, cols] * inverse).astype(jnp.bfloat16).astype(jnp.float32)
             code[:, cols] = c
-            by_row[pl.ds(p * rows * part + t, rows, stride=part), :] = c
+            by_row[pl.ds(p * (rows - 1) * part + t, rows, stride=part), :] = c
+            return held
+
+        over_tiles(p * part, part, code_tile)
         if p == 0:
             pl.semaphore_wait(barrier, n - 1 + groups - 1)
         for k, to in mates.items():
@@ -95,9 +111,11 @@
             for k, to in mates.items():
                 push(scale_send.at[to], scale_got.at[k - 1], scale_sem, (grp, to))
 
-    for t in range(tiles):
-        cols = slice(t * LANES, (t + 1) * LANES)
+    def error_tile(t, cols, held):
         werr_out[:, cols] = blend[:, cols] - scale * code[:, cols]
+        return held
+
+    over_tiles(0, tiles, error_tile)
     loads[3].wait()
 
     wait_bytes(scale_got, scale_sem.at[1])
@@ -139,9 +157,12 @@
         base = p * rows * part
         for r in range(n):
             by_row[base + r * part : base + (r + 1) * part, :] = gathered[p, r].astype(jnp.float32)
-        for t in range(part):
-            cols = slice((p * part + t) * LANES, (p * part + t + 1) * LANES)
-            synced[:, cols] = by_row[pl.ds(base + t, rows, stride=part), :]
+
+        def synced_tile(t, cols, held):
+            synced[:, cols] = by_row[pl.ds(base - p * part + t, rows, stride=part), :]
+            return held
+
+        over_tiles(p * part, part, synced_tile)
 
     wait_bytes(scale_got, scale_sem.at[0])
     for p in range(parts):

time: 18.4 us -> 18.4 us (level)
  no operation moved by 1% of the time
where the time goes in v5:
time: 18.4 us; the launch traced here: 18.3 us
  Pallas kernels  17.6 us (96%)
  between operations  0.64 us (3%)
    pallas_call x1, Pallas kernels, per_device(): pl.pallas_call(functools.partial(kernel, n, groups, rows, width, parts),...  16.8 us
    pallas_call x1, Pallas kernels, per_device(): pl.pallas_call(store, out_shape=tuple((jax.ShapeDtypeStruct(x.shape, f32)...  0.82 us

profile of v5, /device:TPU:0, one launch (start us, length us, event | category | flops | bytes accessed | tf_op | source)
XLA Modules:
  0.0 18.3 jit_solution(6457908360098002468)
XLA Ops:
  0.6 16.8 %sync.1 = (f32[8,8192]{1,0:T(8,128)S(1)}, f32[8,8192]{1,0:T(8,128)S(1)}, f32[64,128]{1,0:T(8,128)S(1)}) custom-call(bf16[8,8192]{1,0:T(8,128)(2,1)} %bitcast.8, f32[8,8192]{1,0:T(8,128)} %bitcast.6, f32[8,8192]{1,0:T(8,128)} %bitcast.7, f32[64,128]{1,0:T(8,128)} %bitcast.9), custom_call_target="tpu_custom_call" | custom-call | tf_op jit(solution)/shard_map/sync/pallas_call | solution.py:202
  17.4 0.8 %store.1 = (f32[8,8192]{1,0:T(8,128)}, f32[8,8192]{1,0:T(8,128)}, f32[64,128]{1,0:T(8,128)}) custom-call(f32[8,8192]{1,0:T(8,128)S(1)} %get-tuple-element.9.synced, f32[8,8192]{1,0:T(8,128)S(1)} %get-tuple-element.10.werr, f32[64,128]{1,0:T(8,128)S(1)} %get-tuple-element.11.serr), custom_call_target="tpu_custom_call" | custom-call | tf_op jit(solution)/shard_map/store/pallas_call | solution.py:242

commit v6 on v5

--- a/solution.py
+++ b/solution.py
@@ -16,7 +16,11 @@
     if n & (n - 1):
         return {k: lax.rem(me + k, n) for k in range(n - 1, 0, -1)}
     flips = [(1 << i, (1 << i) * (1 - 2 * lax.rem(lax.div(me, 1 << i), 2))) for i in range(n.bit_length() - 1)]
-    return {k: me + sum(step for bit, step in flips if k & bit) for k in range(n - 1, 0, -1)}
+    far = list(range(n - 1, 0, -1))
+    half = n // 4
+    near = far[: 2 * half]
+    order = [k for pair in zip(near[:half], near[half:]) for k in pair] + far[2 * half :]
+    return {k: me + sum(step for bit, step in flips if k & bit) for k in order}
 
 
 def over_tiles(start, count, body, carry=0):
@@ -36,7 +40,7 @@
 
 
 def kernel(
-    n, groups, rows, width, parts,
+    n, groups, rows, width, parts, z_parts,
     grads, momentum, worker_error, server_error,
     synced, werr_out, serr_out,
     g_in, m_in, e_in, se_in, blend, code, by_row, entry,
@@ -45,7 +49,7 @@
 ):
     me, grp = lax.axis_index("dp"), lax.axis_index("grp")
     tiles = width // LANES
-    part = tiles // parts
+    part, z_part = tiles // parts, tiles // z_parts
 
     loads = [
         pltpu.make_async_copy(src, dst, in_sem.at[i])
@@ -133,8 +137,8 @@
     mean = jnp.sum(jnp.sum(size, axis=0, keepdims=True), axis=1, keepdims=True) / width
     s_scale = (mean + 1e-6).astype(jnp.bfloat16).astype(jnp.float32)
     s_inverse = 1.0 / s_scale
-    for p in range(parts):
-        here = slice(p * part, (p + 1) * part)
+    for p in range(z_parts):
+        here = slice(p * z_part, (p + 1) * z_part)
         s_code = jnp.tanh(entry[here, :] * s_inverse).astype(jnp.bfloat16).astype(jnp.float32)
         decoded = s_scale * s_code
         zbuf[p, grp] = decoded.astype(jnp.bfloat16)
@@ -142,7 +146,7 @@
             push(zbuf.at[p, grp], zbuf.at[p, grp], z_sem.at[p], (to, me))
         serr_out[here, :] = entry[here, :] - decoded
 
-    for p in range(parts):
+    for p in range(z_parts):
         if groups > 1:
             wait_bytes(zbuf.at[p, pl.ds(0, groups - 1)], z_sem.at[p, 1])
         mixed = zbuf[p, 0].astype(jnp.float32)
@@ -152,21 +156,22 @@
         for to in mates.values():
             push(gathered.at[p, me], gathered.at[p, me], ag_sem.at[p], (grp, to))
 
-    for p in range(parts):
+    for p in range(z_parts):
         wait_bytes(gathered.at[p, pl.ds(0, n - 1)], ag_sem.at[p, 1])
-        base = p * rows * part
+        base = p * rows * z_part
         for r in range(n):
-            by_row[base + r * part : base + (r + 1) * part, :] = gathered[p, r].astype(jnp.float32)
+            by_row[base + r * z_part : base + (r + 1) * z_part, :] = gathered[p, r].astype(jnp.float32)
 
         def synced_tile(t, cols, held):
-            synced[:, cols] = by_row[pl.ds(base - p * part + t, rows, stride=part), :]
+            synced[:, cols] = by_row[pl.ds(base - p * z_part + t, rows, stride=z_part), :]
             return held
 
-        over_tiles(p * part, part, synced_tile)
+        over_tiles(p * z_part, z_part, synced_tile)
 
     wait_bytes(scale_got, scale_sem.at[0])
     for p in range(parts):
         wait_bytes(got.at[p], code_sem.at[p, 0])
+    for p in range(z_parts):
         if groups > 1:
             wait_bytes(zbuf.at[p, pl.ds(0, groups - 1)], z_sem.at[p, 0])
         wait_bytes(gathered.at[p, pl.ds(0, n - 1)], ag_sem.at[p, 0])
@@ -190,8 +195,9 @@
         rows, width = grads.shape[2:]
         assert rows == n
         tiles = width // LANES
-        parts = 2
+        parts, z_parts = 2, 4
         part_block = (tiles // parts, LANES)
+        z_block = (tiles // z_parts, LANES)
         f32, bf16 = jnp.float32, jnp.bfloat16
         whole = (rows, width)
         block = (tiles, LANES)
@@ -200,7 +206,7 @@
         anywhere = pl.BlockSpec(memory_space=pl.ANY)
         pinned = functools.partial(pltpu.with_memory_space_constraint, memory_space=pltpu.HBM)
         synced, werr, serr = pl.pallas_call(
-            functools.partial(kernel, n, groups, rows, width, parts),
+            functools.partial(kernel, n, groups, rows, width, parts, z_parts),
             out_shape=(
                 jax.ShapeDtypeStruct(whole, f32),
                 jax.ShapeDtypeStruct(whole, f32),
@@ -221,13 +227,13 @@
                 pltpu.VMEM((parts, n - 1) + part_block, bf16),
                 pltpu.VMEM((n, 1, LANES), f32),
                 pltpu.VMEM((n - 1, 1, LANES), f32),
-                pltpu.VMEM((parts, groups) + part_block, bf16),
-                pltpu.VMEM((parts, n) + part_block, bf16),
+                pltpu.VMEM((z_parts, groups) + z_block, bf16),
+                pltpu.VMEM((z_parts, n) + z_block, bf16),
                 pltpu.SemaphoreType.DMA((4,)),
                 pltpu.SemaphoreType.DMA((parts, 2)),
                 pltpu.SemaphoreType.DMA((2,)),
-                pltpu.SemaphoreType.DMA((parts, 2)),
-                pltpu.SemaphoreType.DMA((parts, 2)),
+                pltpu.SemaphoreType.DMA((z_parts, 2)),
+                pltpu.SemaphoreType.DMA((z_parts, 2)),
             ],
             compiler_params=pltpu.CompilerParams(
                 collective_id=0, has_side_effects=True, vmem_limit_bytes=48 * 2**20

time: 18.4 us -> 18.4 us (level)
  no operation moved by 1% of the time
where the time goes in v6:
time: 18.4 us; the launch traced here: 18.3 us
  Pallas kernels  17.7 us (96%)
  between operations  0.64 us (3%)
    pallas_call x1, Pallas kernels, per_device(): pl.pallas_call(functools.partial(kernel, n, groups, rows, width, parts, z...  16.8 us
    pallas_call x1, Pallas kernels, per_device(): pl.pallas_call(store, out_shape=tuple((jax.ShapeDtypeStruct(x.shape, f32)...  0.82 us

profile of v6, /device:TPU:0, one launch (start us, length us, event | category | flops | bytes accessed | tf_op | source)
XLA Modules:
  0.0 18.3 jit_solution(7122884839369553046)
XLA Ops:
  0.6 16.8 %sync.1 = (f32[8,8192]{1,0:T(8,128)S(1)}, f32[8,8192]{1,0:T(8,128)S(1)}, f32[64,128]{1,0:T(8,128)S(1)}) custom-call(bf16[8,8192]{1,0:T(8,128)(2,1)} %bitcast.8, f32[8,8192]{1,0:T(8,128)} %bitcast.6, f32[8,8192]{1,0:T(8,128)} %bitcast.7, f32[64,128]{1,0:T(8,128)} %bitcast.9), custom_call_target="tpu_custom_call" | custom-call | tf_op jit(solution)/shard_map/sync/pallas_call | solution.py:208
  17.5 0.8 %store.1 = (f32[8,8192]{1,0:T(8,128)}, f32[8,8192]{1,0:T(8,128)}, f32[64,128]{1,0:T(8,128)}) custom-call(f32[8,8192]{1,0:T(8,128)S(1)} %get-tuple-element.9.synced, f32[8,8192]{1,0:T(8,128)S(1)} %get-tuple-element.10.werr, f32[64,128]{1,0:T(8,128)S(1)} %get-tuple-element.11.serr), custom_call_target="tpu_custom_call" | custom-call | tf_op jit(solution)/shard_map/store/pallas_call | solution.py:248

commit v7 on v6

--- a/solution.py
+++ b/solution.py
@@ -57,9 +57,6 @@
             ((momentum, m_in), (worker_error, e_in), (grads, g_in), (server_error, se_in))
         )
     ]
-    for load in loads:
-        load.start()
-
     mates = partners(me, n)
     others = partners(grp, groups)
     barrier = pltpu.get_barrier_semaphore()
@@ -67,6 +64,8 @@
         pl.semaphore_signal(barrier, inc=1, device_id=(grp, to), device_id_type=MESH)
     for to in others.values():
         pl.semaphore_signal(barrier, inc=1, device_id=(to, me), device_id_type=MESH)
+    for load in loads:
+        load.start()
 
     def push(src, dst, sems, device):
         pltpu.make_async_remote_copy(
@@ -106,14 +105,15 @@
             return held
 
         over_tiles(p * part, part, code_tile)
-        if p == 0:
-            pl.semaphore_wait(barrier, n - 1 + groups - 1)
         for k, to in mates.items():
             send[p, k - 1] = by_row[block_of(p, to), :].astype(jnp.bfloat16)
+
+    pl.semaphore_wait(barrier, n - 1 + groups - 1)
+    for p in range(parts):
+        for k, to in mates.items():
             push(send.at[p, k - 1], got.at[p, k - 1], code_sem.at[p], (grp, to))
-        if p == 0:
-            for k, to in mates.items():
-                push(scale_send.at[to], scale_got.at[k - 1], scale_sem, (grp, to))
+    for k, to in mates.items():
+        push(scale_send.at[to], scale_got.at[k - 1], scale_sem, (grp, to))
 
     def error_tile(t, cols, held):
         werr_out[:, cols] = blend[:, cols] - scale * code[:, cols]
@@ -195,7 +195,7 @@
         rows, width = grads.shape[2:]
         assert rows == n
         tiles = width // LANES
-        parts, z_parts = 2, 4
+        parts, z_parts = 1, 2
         part_block = (tiles // parts, LANES)
         z_block = (tiles // z_parts, LANES)
         f32, bf16 = jnp.float32, jnp.bfloat16

time: 18.4 us -> 18.5 us (level)
  no operation moved by 1% of the time
where the time goes in v7:
time: 18.5 us; the launch traced here: 18.4 us
  Pallas kernels  17.7 us (96%)
  between operations  0.64 us (3%)
    pallas_call x1, Pallas kernels, per_device(): pl.pallas_call(functools.partial(kernel, n, groups, rows, width, parts, z...  16.9 us
    pallas_call x1, Pallas kernels, per_device(): pl.pallas_call(store, out_shape=tuple((jax.ShapeDtypeStruct(x.shape, f32)...  0.82 us

profile of v7, /device:TPU:0, one launch (start us, length us, event | category | flops | bytes accessed | tf_op | source)
XLA Modules:
  0.0 18.4 jit_solution(7242758835572895998)
XLA Ops:
  0.6 16.9 %sync.1 = (f32[8,8192]{1,0:T(8,128)S(1)}, f32[8,8192]{1,0:T(8,128)S(1)}, f32[64,128]{1,0:T(8,128)S(1)}) custom-call(bf16[8,8192]{1,0:T(8,128)(2,1)} %bitcast.8, f32[8,8192]{1,0:T(8,128)} %bitcast.6, f32[8,8192]{1,0:T(8,128)} %bitcast.7, f32[64,128]{1,0:T(8,128)} %bitcast.9), custom_call_target="tpu_custom_call" | custom-call | tf_op jit(solution)/shard_map/sync/pallas_call | solution.py:208
  17.6 0.8 %store.1 = (f32[8,8192]{1,0:T(8,128)}, f32[8,8192]{1,0:T(8,128)}, f32[64,128]{1,0:T(8,128)}) custom-call(f32[8,8192]{1,0:T(8,128)S(1)} %get-tuple-element.9.synced, f32[8,8192]{1,0:T(8,128)S(1)} %get-tuple-element.10.werr, f32[64,128]{1,0:T(8,128)S(1)} %get-tuple-element.11.serr), custom_call_target="tpu_custom_call" | custom-call | tf_op jit(solution)/shard_map/store/pallas_call | solution.py:248

commit v8 on v7

--- a/solution.py
+++ b/solution.py
@@ -43,9 +43,9 @@
     n, groups, rows, width, parts, z_parts,
     grads, momentum, worker_error, server_error,
     synced, werr_out, serr_out,
-    g_in, m_in, e_in, se_in, blend, code, by_row, entry,
-    send, got, scale_send, scale_got, zbuf, gathered,
-    in_sem, code_sem, scale_sem, z_sem, ag_sem,
+    g_in, m_in, e_in, se_in, blend, decoded_in, by_row, entry,
+    send, got, zbuf, gathered,
+    in_sem, row_sem, z_sem, ag_sem,
 ):
     me, grp = lax.axis_index("dp"), lax.axis_index("grp")
     tiles = width // LANES
@@ -90,47 +90,42 @@
     scale = (mean + 1e-6).astype(jnp.bfloat16).astype(jnp.float32)
     inverse = jnp.broadcast_to(1.0 / scale, (rows, LANES))
     scale = jnp.broadcast_to(scale, (rows, LANES))
-    for r in range(rows):
-        scale_send[r] = scale[r : r + 1]
 
     def block_of(p, r):
         return pl.ds(pl.multiple_of((p * rows + r) * part, part), part)
 
     for p in range(parts):
 
-        def code_tile(t, cols, held):
+        def decode_tile(t, cols, held):
             c = jnp.tanh(blend[:, cols] * inverse).astype(jnp.bfloat16).astype(jnp.float32)
-            code[:, cols] = c
+            c = scale * c
+            decoded_in[:, cols] = c
             by_row[pl.ds(p * (rows - 1) * part + t, rows, stride=part), :] = c
             return held
 
-        over_tiles(p * part, part, code_tile)
+        over_tiles(p * part, part, decode_tile)
         for k, to in mates.items():
             send[p, k - 1] = by_row[block_of(p, to), :].astype(jnp.bfloat16)
 
     pl.semaphore_wait(barrier, n - 1 + groups - 1)
     for p in range(parts):
         for k, to in mates.items():
-            push(send.at[p, k - 1], got.at[p, k - 1], code_sem.at[p], (grp, to))
-    for k, to in mates.items():
-        push(scale_send.at[to], scale_got.at[k - 1], scale_sem, (grp, to))
+            push(send.at[p, k - 1], got.at[p, k - 1], row_sem.at[p], (grp, to))
 
     def error_tile(t, cols, held):
-        werr_out[:, cols] = blend[:, cols] - scale * code[:, cols]
+        werr_out[:, cols] = blend[:, cols] - decoded_in[:, cols]
         return held
 
     over_tiles(0, tiles, error_tile)
     loads[3].wait()
 
-    wait_bytes(scale_got, scale_sem.at[1])
-    heights = [scale_got[k] for k in range(n - 1)]
     size = jnp.zeros((part, LANES), jnp.float32)
     for p in range(parts):
         here = slice(p * part, (p + 1) * part)
-        summed = by_row[block_of(p, me), :] * scale_send[me]
-        wait_bytes(got.at[p], code_sem.at[p, 1])
+        summed = by_row[block_of(p, me), :]
+        wait_bytes(got.at[p], row_sem.at[p, 1])
         for k in range(n - 1):
-            summed = summed + got[p, k].astype(jnp.float32) * heights[k]
+            summed = summed + got[p, k].astype(jnp.float32)
         summed = summed / n + se_in[here, :]
         entry[here, :] = summed
         size = size + jnp.abs(summed)
@@ -168,9 +163,8 @@
 
         over_tiles(p * z_part, z_part, synced_tile)
 
-    wait_bytes(scale_got, scale_sem.at[0])
-    for p in range(parts):
-        wait_bytes(got.at[p], code_sem.at[p, 0])
+    for p in range(parts):
+        wait_bytes(got.at[p], row_sem.at[p, 0])
     for p in range(z_parts):
         if groups > 1:
             wait_bytes(zbuf.at[p, pl.ds(0, groups - 1)], z_sem.at[p, 0])
@@ -225,13 +219,10 @@
                 pltpu.VMEM(block, f32),
                 pltpu.VMEM((parts, n - 1) + part_block, bf16),
                 pltpu.VMEM((parts, n - 1) + part_block, bf16),
-                pltpu.VMEM((n, 1, LANES), f32),
-                pltpu.VMEM((n - 1, 1, LANES), f32),
                 pltpu.VMEM((z_parts, groups) + z_block, bf16),
                 pltpu.VMEM((z_parts, n) + z_block, bf16),
                 pltpu.SemaphoreType.DMA((4,)),
                 pltpu.SemaphoreType.DMA((parts, 2)),
-                pltpu.SemaphoreType.DMA((2,)),
                 pltpu.SemaphoreType.DMA((z_parts, 2)),
                 pltpu.SemaphoreType.DMA((z_parts, 2)),
             ],

time: 18.5 us -> 18.1 us (0.978)
  Pallas kernels: 17.7 us -> 17.4 us
    pallas_call x1, Pallas kernels: 16.9 us -> 16.5 us  [per_device(): pl.pallas_call(functools.partial(kernel, n, groups, rows, width, parts, z...]
where the time goes in v8:
time: 18.1 us; the launch traced here: 18 us
  Pallas kernels  17.4 us (96%)
  between operations  0.64 us (4%)
    pallas_call x1, Pallas kernels, per_device(): pl.pallas_call(functools.partial(kernel, n, groups, rows, width, parts, z...  16.5 us
    pallas_call x1, Pallas kernels, per_device(): pl.pallas_call(store, out_shape=tuple((jax.ShapeDtypeStruct(x.shape, f32)...  0.82 us

profile of v8, /device:TPU:0, one launch (start us, length us, event | category | flops | bytes accessed | tf_op | source)
XLA Modules:
  0.0 18.0 jit_solution(8058577834918465406)
XLA Ops:
  0.6 16.5 %sync.1 = (f32[8,8192]{1,0:T(8,128)S(1)}, f32[8,8192]{1,0:T(8,128)S(1)}, f32[64,128]{1,0:T(8,128)S(1)}) custom-call(bf16[8,8192]{1,0:T(8,128)(2,1)} %bitcast.8, f32[8,8192]{1,0:T(8,128)} %bitcast.6, f32[8,8192]{1,0:T(8,128)} %bitcast.7, f32[64,128]{1,0:T(8,128)} %bitcast.9), custom_call_target="tpu_custom_call" | custom-call | tf_op jit(solution)/shard_map/sync/pallas_call | solution.py:202
  17.2 0.8 %store.1 = (f32[8,8192]{1,0:T(8,128)}, f32[8,8192]{1,0:T(8,128)}, f32[64,128]{1,0:T(8,128)}) custom-call(f32[8,8192]{1,0:T(8,128)S(1)} %get-tuple-element.9.synced, f32[8,8192]{1,0:T(8,128)S(1)} %get-tuple-element.10.werr, f32[64,128]{1,0:T(8,128)S(1)} %get-tuple-element.11.serr), custom_call_target="tpu_custom_call" | custom-call | tf_op jit(solution)/shard_map/store/pallas_call | solution.py:239

commit v9 on v8

--- a/solution.py
+++ b/solution.py
@@ -51,12 +51,25 @@
     tiles = width // LANES
     part, z_part = tiles // parts, tiles // z_parts
 
+    halves = 2
+    half = width // halves
+    grads_load = pltpu.make_async_copy(grads, g_in, in_sem.at[0])
+    server_load = pltpu.make_async_copy(server_error, se_in, in_sem.at[1])
     loads = [
-        pltpu.make_async_copy(src, dst, in_sem.at[i])
-        for i, (src, dst) in enumerate(
-            ((momentum, m_in), (worker_error, e_in), (grads, g_in), (server_error, se_in))
-        )
+        [
+            pltpu.make_async_copy(
+                src.at[:, pl.ds(h * half, half)], dst.at[:, pl.ds(h * half, half)], in_sem.at[2 + 2 * h + i]
+            )
+            for i, (src, dst) in enumerate(((momentum, m_in), (worker_error, e_in)))
+        ]
+        for h in range(halves)
     ]
+    grads_load.start()
+    for pair in loads:
+        for load in pair:
+            load.start()
+    server_load.start()
+
     mates = partners(me, n)
     others = partners(grp, groups)
     barrier = pltpu.get_barrier_semaphore()
@@ -64,8 +77,6 @@
         pl.semaphore_signal(barrier, inc=1, device_id=(grp, to), device_id_type=MESH)
     for to in others.values():
         pl.semaphore_signal(barrier, inc=1, device_id=(to, me), device_id_type=MESH)
-    for load in loads:
-        load.start()
 
     def push(src, dst, sems, device):
         pltpu.make_async_remote_copy(
@@ -77,15 +88,17 @@
             device_id_type=MESH,
         ).start()
 
-    for load in loads[:3]:
-        load.wait()
-
     def blend_tile(t, cols, total):
         b = 0.9 * m_in[:, cols] + 0.1 * g_in[:, cols].astype(jnp.float32) + e_in[:, cols]
         blend[:, cols] = b
         return total + jnp.abs(b)
 
-    total = over_tiles(0, tiles, blend_tile, jnp.zeros((rows, LANES), jnp.float32))
+    total = jnp.zeros((rows, LANES), jnp.float32)
+    grads_load.wait()
+    for h, pair in enumerate(loads):
+        for load in pair:
+            load.wait()
+        total = over_tiles(h * (tiles // halves), tiles // halves, blend_tile, total)
     mean = jnp.sum(total, axis=1, keepdims=True) / width
     scale = (mean + 1e-6).astype(jnp.bfloat16).astype(jnp.float32)
     inverse = jnp.broadcast_to(1.0 / scale, (rows, LANES))
@@ -117,7 +130,7 @@
         return held
 
     over_tiles(0, tiles, error_tile)
-    loads[3].wait()
+    server_load.wait()
 
     size = jnp.zeros((part, LANES), jnp.float32)
     for p in range(parts):
@@ -151,6 +164,12 @@
         for to in mates.values():
             push(gathered.at[p, me], gathered.at[p, me], ag_sem.at[p], (grp, to))
 
+    for p in range(parts):
+        wait_bytes(got.at[p], row_sem.at[p, 0])
+    if groups > 1:
+        for p in range(z_parts):
+            wait_bytes(zbuf.at[p, pl.ds(0, groups - 1)], z_sem.at[p, 0])
+
     for p in range(z_parts):
         wait_bytes(gathered.at[p, pl.ds(0, n - 1)], ag_sem.at[p, 1])
         base = p * rows * z_part
@@ -163,11 +182,7 @@
 
         over_tiles(p * z_part, z_part, synced_tile)
 
-    for p in range(parts):
-        wait_bytes(got.at[p], row_sem.at[p, 0])
-    for p in range(z_parts):
-        if groups > 1:
-            wait_bytes(zbuf.at[p, pl.ds(0, groups - 1)], z_sem.at[p, 0])
+    for p in range(z_parts):
         wait_bytes(gathered.at[p, pl.ds(0, n - 1)], ag_sem.at[p, 0])
 
 
@@ -221,7 +236,7 @@
                 pltpu.VMEM((parts, n - 1) + part_block, bf16),
                 pltpu.VMEM((z_parts, groups) + z_block, bf16),
                 pltpu.VMEM((z_parts, n) + z_block, bf16),
-                pltpu.SemaphoreType.DMA((4,)),
+                pltpu.SemaphoreType.DMA((6,)),
                 pltpu.SemaphoreType.DMA((parts, 2)),
                 pltpu.SemaphoreType.DMA((z_parts, 2)),
                 pltpu.SemaphoreType.DMA((z_parts, 2)),

time: 18.1 us -> 18.2 us (level)
  no operation moved by 1% of the time
where the time goes in v9:
time: 18.2 us; the launch traced here: 18 us
  Pallas kernels  17.4 us (96%)
  between operations  0.64 us (4%)
    pallas_call x1, Pallas kernels, per_device(): pl.pallas_call(functools.partial(kernel, n, groups, rows, width, parts, z...  16.6 us
    pallas_call x1, Pallas kernels, per_device(): pl.pallas_call(store, out_shape=tuple((jax.ShapeDtypeStruct(x.shape, f32)...  0.82 us

profile of v9, /device:TPU:0, one launch (start us, length us, event | category | flops | bytes accessed | tf_op | source)
XLA Modules:
  0.0 18.0 jit_solution(7508987754118661688)
XLA Ops:
  0.6 16.6 %sync.1 = (f32[8,8192]{1,0:T(8,128)S(1)}, f32[8,8192]{1,0:T(8,128)S(1)}, f32[64,128]{1,0:T(8,128)S(1)}) custom-call(bf16[8,8192]{1,0:T(8,128)(2,1)} %bitcast.8, f32[8,8192]{1,0:T(8,128)} %bitcast.6, f32[8,8192]{1,0:T(8,128)} %bitcast.7, f32[64,128]{1,0:T(8,128)} %bitcast.9), custom_call_target="tpu_custom_call" | custom-call | tf_op jit(solution)/shard_map/sync/pallas_call | solution.py:217
  17.2 0.8 %store.1 = (f32[8,8192]{1,0:T(8,128)}, f32[8,8192]{1,0:T(8,128)}, f32[64,128]{1,0:T(8,128)}) custom-call(f32[8,8192]{1,0:T(8,128)S(1)} %get-tuple-element.9.synced, f32[8,8192]{1,0:T(8,128)S(1)} %get-tuple-element.10.werr, f32[64,128]{1,0:T(8,128)S(1)} %get-tuple-element.11.serr), custom_call_target="tpu_custom_call" | custom-call | tf_op jit(solution)/shard_map/store/pallas_call | solution.py:254

commit v10 on v9

--- a/solution.py
+++ b/solution.py
@@ -204,7 +204,7 @@
         rows, width = grads.shape[2:]
         assert rows == n
         tiles = width // LANES
-        parts, z_parts = 1, 2
+        parts, z_parts = 1, 1
         part_block = (tiles // parts, LANES)
         z_block = (tiles // z_parts, LANES)
         f32, bf16 = jnp.float32, jnp.bfloat16

time: 18.2 us -> 18.2 us (level)
  no operation moved by 1% of the time
where the time goes in v10:
time: 18.2 us; the launch traced here: 18 us
  Pallas kernels  17.4 us (96%)
  between operations  0.64 us (4%)
    pallas_call x1, Pallas kernels, per_device(): pl.pallas_call(functools.partial(kernel, n, groups, rows, width, parts, z...  16.6 us
    pallas_call x1, Pallas kernels, per_device(): pl.pallas_call(store, out_shape=tuple((jax.ShapeDtypeStruct(x.shape, f32)...  0.82 us

profile of v10, /device:TPU:0, one launch (start us, length us, event | category | flops | bytes accessed | tf_op | source)
XLA Modules:
  0.0 18.0 jit_solution(11818830265067573546)
XLA Ops:
  0.6 16.6 %sync.1 = (f32[8,8192]{1,0:T(8,128)S(1)}, f32[8,8192]{1,0:T(8,128)S(1)}, f32[64,128]{1,0:T(8,128)S(1)}) custom-call(bf16[8,8192]{1,0:T(8,128)(2,1)} %bitcast.8, f32[8,8192]{1,0:T(8,128)} %bitcast.6, f32[8,8192]{1,0:T(8,128)} %bitcast.7, f32[64,128]{1,0:T(8,128)} %bitcast.9), custom_call_target="tpu_custom_call" | custom-call | tf_op jit(solution)/shard_map/sync/pallas_call | solution.py:217
  17.2 0.8 %store.1 = (f32[8,8192]{1,0:T(8,128)}, f32[8,8192]{1,0:T(8,128)}, f32[64,128]{1,0:T(8,128)}) custom-call(f32[8,8192]{1,0:T(8,128)S(1)} %get-tuple-element.9.synced, f32[8,8192]{1,0:T(8,128)S(1)} %get-tuple-element.10.werr, f32[64,128]{1,0:T(8,128)S(1)} %get-tuple-element.11.serr), custom_call_target="tpu_custom_call" | custom-call | tf_op jit(solution)/shard_map/store/pallas_call | solution.py:254

commit v11 on v10

--- a/solution.py
+++ b/solution.py
@@ -64,12 +64,6 @@
         ]
         for h in range(halves)
     ]
-    grads_load.start()
-    for pair in loads:
-        for load in pair:
-            load.start()
-    server_load.start()
-
     mates = partners(me, n)
     others = partners(grp, groups)
     barrier = pltpu.get_barrier_semaphore()
@@ -77,6 +71,11 @@
         pl.semaphore_signal(barrier, inc=1, device_id=(grp, to), device_id_type=MESH)
     for to in others.values():
         pl.semaphore_signal(barrier, inc=1, device_id=(to, me), device_id_type=MESH)
+    grads_load.start()
+    for pair in loads:
+        for load in pair:
+            load.start()
+    server_load.start()
 
     def push(src, dst, sems, device):
         pltpu.make_async_remote_copy(
@@ -230,7 +229,7 @@
                 pltpu.VMEM(block, f32),
                 pltpu.VMEM(whole, f32),
                 pltpu.VMEM(whole, f32),
-                pltpu.VMEM((rows * tiles, LANES), f32),
+                pltpu.VMEM(((rows + 1) * tiles, LANES), f32),
                 pltpu.VMEM(block, f32),
                 pltpu.VMEM((parts, n - 1) + part_block, bf16),
                 pltpu.VMEM((parts, n - 1) + part_block, bf16),

time: 18.2 us -> 18.2 us (level)
  no operation moved by 1% of the time
where the time goes in v11:
time: 18.2 us; the launch traced here: 18 us
  Pallas kernels  17.4 us (96%)
  between operations  0.64 us (4%)
    pallas_call x1, Pallas kernels, per_device(): pl.pallas_call(functools.partial(kernel, n, groups, rows, width, parts, z...  16.6 us
    pallas_call x1, Pallas kernels, per_device(): pl.pallas_call(store, out_shape=tuple((jax.ShapeDtypeStruct(x.shape, f32)...  0.82 us

profile of v11, /device:TPU:0, one launch (start us, length us, event | category | flops | bytes accessed | tf_op | source)
XLA Modules:
  0.0 18.0 jit_solution(10702779507720924999)
XLA Ops:
  0.6 16.6 %sync.1 = (f32[8,8192]{1,0:T(8,128)S(1)}, f32[8,8192]{1,0:T(8,128)S(1)}, f32[64,128]{1,0:T(8,128)S(1)}) custom-call(bf16[8,8192]{1,0:T(8,128)(2,1)} %bitcast.8, f32[8,8192]{1,0:T(8,128)} %bitcast.6, f32[8,8192]{1,0:T(8,128)} %bitcast.7, f32[64,128]{1,0:T(8,128)} %bitcast.9), custom_call_target="tpu_custom_call" | custom-call | tf_op jit(solution)/shard_map/sync/pallas_call | solution.py:216
  17.2 0.8 %store.1 = (f32[8,8192]{1,0:T(8,128)}, f32[8,8192]{1,0:T(8,128)}, f32[64,128]{1,0:T(8,128)}) custom-call(f32[8,8192]{1,0:T(8,128)S(1)} %get-tuple-element.9.synced, f32[8,8192]{1,0:T(8,128)S(1)} %get-tuple-element.10.werr, f32[64,128]{1,0:T(8,128)S(1)} %get-tuple-element.11.serr), custom_call_target="tpu_custom_call" | custom-call | tf_op jit(solution)/shard_map/store/pallas_call | solution.py:253
